TPU v7x, 512 devices: a whole 4x4x16 slice. The times are simulated.
512 devices in a mesh: seq: 32 (over z_lo, x), head: 16 (over y, z_hi, core).
Axes of the slice: x: 4, y: 4, z: 16 (z_hi: 2, z_lo: 8; z = z_hi * 8 + z_lo), core: 2. Of those that a mesh axis runs over, the one named last changes fastest.
Arguments:
- queries: bfloat16 [32768, 4096], P(('seq', 'head'))
- keys: bfloat16 [32768, 2048], P(('seq', 'head'))
- values: bfloat16 [32768, 2048], P(('seq', 'head')), may hold values from -6 to 6
- dout: bfloat16 [32768, 4096], P(('seq', 'head')), may hold values from -6 to 6
- doc_starts: int32 [32], replicated, may hold values from 0 to 32767, as said below
Outputs:
- dquery: bfloat16 [32768, 4096], P(('seq', 'head'))
- dkey: bfloat16 [32768, 2048], P(('seq', 'head'))
- dvalue: bfloat16 [32768, 2048], P(('seq', 'head'))
Inputs may be any that keep to these rules, and one draw needn't show every extreme that they name: doc_starts[0] = 0, strictly increasing.
All inputs are finite; a program needn't handle non-finite values.
Results may differ from a plain program's by a relative error of at most 0.03.
Values may be sent and summed in bfloat16 or wider, within the bound.
A program may use at most 64 MiB of HBM per device.

v0:
```python
import jax
import jax.numpy as jnp
from jax import lax
from jax.sharding import PartitionSpec as P

HEAD_SIZE = 128
WINDOW_LENGTH = 512


scale_factor = 168.0 ** (-0.5)
negative = -1e30


def passed_along(x, axis, by):
    length = lax.axis_size(axis)
    pairs = [(i, i + by) for i in range(length) if 0 <= i + by < length]
    return lax.ppermute(x, axis, pairs)


def doc_ids(positions, doc_starts):
    return jnp.sum((doc_starts[None, :] <= positions[:, None]).astype(jnp.int32), axis=1) - 1


def allowed_pairs(query_pos, key_pos, doc_starts, limit, window):
    query_doc = doc_ids(query_pos, doc_starts)
    key_doc = doc_ids(key_pos, doc_starts)
    return (
        (key_pos[None, :] >= 0)
        & (key_pos[None, :] <= query_pos[:, None])
        & (query_pos[:, None] - key_pos[None, :] < window)
        & (query_doc[:, None] == key_doc[None, :])
        & (query_pos[:, None] < limit)
    )


def dot_rows(left, right):
    return lax.dot_general(
        left, right, (((1,), (1,)), ((), ())), preferred_element_type=jnp.float32
    )


def dot_cols(left, right):
    return lax.dot_general(
        left, right, (((0,), (0,)), ((), ())), preferred_element_type=jnp.float32
    )


def head_tile(q_blk, g_blk, key_win, value_win, allowed):
    masked = jnp.where(allowed, dot_rows(q_blk, key_win) * scale_factor, negative)
    peak = jnp.max(masked, axis=1, keepdims=True)
    total = jnp.sum(jnp.exp(masked - peak), axis=1, keepdims=True)
    log_sum = peak + jnp.log(total)
    probs = jnp.exp(masked - log_sum)
    probs_low = probs.astype(jnp.bfloat16)
    output = jnp.dot(probs_low, value_win, preferred_element_type=jnp.float32).astype(jnp.bfloat16)
    output = lax.optimization_barrier(output)
    delta = jnp.sum(g_blk.astype(jnp.float32) * output.astype(jnp.float32), axis=1, keepdims=True)
    dprobs = dot_rows(g_blk, value_win)
    dscores = (probs * (dprobs - delta) * scale_factor).astype(jnp.bfloat16)
    dq_blk = jnp.dot(dscores, key_win, preferred_element_type=jnp.float32)
    return (dq_blk, dscores, probs_low, log_sum, delta)


def shards(queries, keys, values, dout, doc_starts):
    q_local, k_local, v_local, g_local = (
        lax.all_to_all(queries, "head", split_axis=1, concat_axis=0, tiled=True),
        lax.all_to_all(keys, "head", split_axis=1, concat_axis=0, tiled=True),
        lax.all_to_all(values, "head", split_axis=1, concat_axis=0, tiled=True),
        lax.all_to_all(dout, "head", split_axis=1, concat_axis=0, tiled=True),
    )
    rows = q_local.shape[0]
    width = k_local.shape[1]
    query_group = q_local.shape[1] // width
    span = WINDOW_LENGTH
    blocks = rows // span
    halo_keys, halo_values = passed_along(
        (k_local[rows - span :], v_local[rows - span :]), "seq", 1
    )
    extended_keys = jnp.concatenate([halo_keys, k_local], axis=0)
    extended_values = jnp.concatenate([halo_values, v_local], axis=0)
    base = lax.axis_index("seq") * rows
    limit = lax.axis_size("seq") * rows
    spread = jnp.arange(span, dtype=jnp.int32)
    double = jnp.arange(2 * span, dtype=jnp.int32)
    skipped = 0
    key_grad = jnp.zeros((rows + span, width), jnp.float32)
    value_grad = jnp.zeros((rows + span, width), jnp.float32)
    dq_rows = []
    first_lse = []
    first_delta = []
    for blk in range(blocks):
        lower = skipped if blk == 0 else 0
        allowed = allowed_pairs(
            base + blk * span + spread, base + (blk - 1) * span + double, doc_starts, limit, span
        )
        row_parts = []
        key_win = extended_keys[blk * span : (blk + 2) * span, 0:HEAD_SIZE]
        value_win = extended_values[blk * span : (blk + 2) * span, 0:HEAD_SIZE]
        key_sum = jnp.zeros((2 * span - lower, HEAD_SIZE), jnp.float32)
        value_sum = jnp.zeros((2 * span - lower, HEAD_SIZE), jnp.float32)
        for member in range(query_group):
            column = member * HEAD_SIZE
            q_blk = q_local[blk * span : (blk + 1) * span, column : column + HEAD_SIZE]
            g_blk = g_local[blk * span : (blk + 1) * span, column : column + HEAD_SIZE]
            dq_blk, dscores, probs_low, log_sum, delta = head_tile(
                q_blk, g_blk, key_win, value_win, allowed
            )
            row_parts.append(dq_blk.astype(jnp.bfloat16))
            if blk == 0:
                first_lse.append(log_sum[:, 0])
                first_delta.append(delta[:, 0])
            key_sum = key_sum + dot_cols(dscores, q_blk)
            value_sum = value_sum + dot_cols(probs_low, g_blk)
        key_grad = key_grad.at[blk * span + lower : (blk + 2) * span, 0:HEAD_SIZE].add(key_sum)
        value_grad = value_grad.at[blk * span + lower : (blk + 2) * span, 0:HEAD_SIZE].add(
            value_sum
        )
        dq_rows.append(jnp.concatenate(row_parts, axis=1))
    dquery_local = jnp.concatenate(dq_rows, axis=0)
    back_keys, back_values = passed_along((key_grad[:span], value_grad[:span]), "seq", -1)
    dkey_local = jnp.concatenate([key_grad[span:rows], key_grad[rows:] + back_keys], axis=0).astype(
        jnp.bfloat16
    )
    dvalue_local = jnp.concatenate(
        [value_grad[span:rows], value_grad[rows:] + back_values], axis=0
    ).astype(jnp.bfloat16)
    dquery, dkey, dvalue = (
        lax.all_to_all(dquery_local, "head", split_axis=0, concat_axis=1, tiled=True),
        lax.all_to_all(dkey_local, "head", split_axis=0, concat_axis=1, tiled=True),
        lax.all_to_all(dvalue_local, "head", split_axis=0, concat_axis=1, tiled=True),
    )
    return (dquery, dkey, dvalue)


def solution(mesh):
    return jax.shard_map(
        shards,
        mesh=mesh,
        in_specs=(
            P(("seq", "head"), None),
            P(("seq", "head"), None),
            P(("seq", "head"), None),
            P(("seq", "head"), None),
            P(),
        ),
        out_specs=(P(("seq", "head"), None), P(("seq", "head"), None), P(("seq", "head"), None)),
        check_vma=False,
    )
```

profile of v0, /device:TPU:193, one launch (start us, length us, event | category | flops | bytes accessed | tf_op | source)
XLA Modules:
  0.0 241.7 jit_solution(6889128186807893065)
XLA Ops:
  0.7 0.9 copy-done
  1.6 0.8 copy_bitcast_fusion.5
  2.4 11.9 %all-to-all-start = ((bf16[64,16,128]{2,0,1:T(8,128)(2,1)}), bf16[64,16,128]{2,0,1:T(8,128)(2,1)S(1)}, u32[]{:S(2)}, u32[]{:S(2)}) async-start(bf16[64,16,128]{2,0,1:T(8,128)(2,1)} %copy_bitcast_fusion.5), calls=%async_computation | async-start | bytes 524288 | tf_op jit(solution)/shard_map/all_to_all | solution.py:67
  14.3 1.7 copy_bitcast_fusion.4
  16.0 22.6 %all-to-all-done = bf16[64,16,128]{2,0,1:T(8,128)(2,1)S(1)} async-done(((bf16[64,16,128]{2,0,1:T(8,128)(2,1)}), bf16[64,16,128]{2,0,1:T(8,128)(2,1)S(1)}, u32[]{:S(2)}, u32[]{:S(2)}) %all-to-all-start) | async-done | bytes 262176 | tf_op jit(solution)/shard_map/all_to_all | solution.py:67
  38.6 4.3 %all-to-all-start.2 = ((bf16[64,16,128]{2,0,1:T(8,128)(2,1)}), bf16[64,16,128]{2,0,1:T(8,128)(2,1)S(1)}, u32[]{:S(2)}, u32[]{:S(2)}) async-start(bf16[64,16,128]{2,0,1:T(8,128)(2,1)} %copy_bitcast_fusion.4), calls=%async_computation.2 | async-start | bytes 524288 | tf_op jit(solution)/shard_map/all_to_all | solution.py:68
  42.9 0.8 copy.80
  43.8 20.1 %all-to-all-done.2 = bf16[64,16,128]{2,0,1:T(8,128)(2,1)S(1)} async-done(((bf16[64,16,128]{2,0,1:T(8,128)(2,1)}), bf16[64,16,128]{2,0,1:T(8,128)(2,1)S(1)}, u32[]{:S(2)}, u32[]{:S(2)}) %all-to-all-start.2) | async-done | bytes 262176 | tf_op jit(solution)/shard_map/all_to_all | solution.py:68
  63.8 3.8 %all-to-all-start.1 = ((bf16[64,16,256]{2,0,1:T(8,128)(2,1)}), bf16[64,16,256]{2,0,1:T(8,128)(2,1)S(1)}, u32[]{:S(2)}, u32[]{:S(2)}) async-start(bf16[64,16,256]{2,0,1:T(8,128)(2,1)} %bitcast.81), calls=%async_computation.1 | async-start | bytes 1048576 | tf_op jit(solution)/shard_map/all_to_all | solution.py:66
  68.0 3.1 %collective-permute-start = (bf16[512,128]{1,0:T(8,128)(2,1)S(1)}, bf16[512,128]{1,0:T(8,128)(2,1)S(1)}, u32[]{:S(2)}, u32[]{:S(2)}) collective-permute-start(bf16[512,128]{1,0:T(8,128)(2,1)S(1)} %bitcast.122), channel_id=1, source_target_pairs={{0,16},{16,32},{32,48},{48,64},{64,80},{80,96},{96,112},{112,128},... | collective-permute-start | bytes 393224 | tf_op jit(solution)/shard_map/ppermute | solution.py:17
  71.2 0.9 copy.79
  72.1 0.7 slice.162
  72.7 3.1 %collective-permute-start.1 = (bf16[512,128]{1,0:T(8,128)(2,1)}, bf16[512,128]{1,0:T(8,128)(2,1)S(1)}, u32[]{:S(2)}, u32[]{:S(2)}) collective-permute-start(bf16[512,128]{1,0:T(8,128)(2,1)} %bitcast.7), channel_id=1, source_target_pairs={{0,16},{16,32},{32,48},{48,64},{64,80},{80,96},{96,112},{112,128},... | collective-permute-start | bytes 393224 | tf_op jit(solution)/shard_map/ppermute | solution.py:17
  75.8 22.5 %all-to-all-done.1 = bf16[64,16,256]{2,0,1:T(8,128)(2,1)S(1)} async-done(((bf16[64,16,256]{2,0,1:T(8,128)(2,1)}), bf16[64,16,256]{2,0,1:T(8,128)(2,1)S(1)}, u32[]{:S(2)}, u32[]{:S(2)}) %all-to-all-start.1) | async-done | bytes 524320 | tf_op jit(solution)/shard_map/all_to_all | solution.py:66
  98.4 3.9 %all-to-all-start.3 = ((bf16[64,16,256]{2,0,1:T(8,128)(2,1)}), bf16[64,16,256]{2,0,1:T(8,128)(2,1)S(1)}, u32[]{:S(2)}, u32[]{:S(2)}) async-start(bf16[64,16,256]{2,0,1:T(8,128)(2,1)} %bitcast.80), calls=%async_computation.3 | async-start | bytes 1048576 | tf_op jit(solution)/shard_map/all_to_all | solution.py:69
  102.2 1.2 fusion.46
  103.4 1.3 copy-done.3
  105.1 1.1 fusion.47
  106.7 1.2 fusion.48
  108.3 0.9 copy-done.5
  109.2 2.6 %fusion.49 = (f32[512]{0:T(512)}, f32[512,1024]{0,1:T(8,128)S(1)}) fusion(bf16[1024,128]{1,0:T(8,128)(2,1)S(1)} %bitcast.104, bf16[1024,256]{1,0:T(8,128)(2,1)} %bitcast.113, pred[512]{0:T(512)(128)(4,1)S(1)} %copy-done.32, s32[1024]{0:T(1024)S(1)} %copy-done.23, s32[512]{0:T(512)S(1)} %copy-done.26, s32[512]{0:T(512)S(1)} %copy-done.20, ...), kind=kOutput, calls=%fused_computation.112 | convolution fusion | flops 139984384 | bytes 2506240 | tf_op jit(solution)/shard_map/dot_general | solution.py:37
  111.8 21.1 %all-to-all-done.3 = bf16[64,16,256]{2,0,1:T(8,128)(2,1)S(1)} async-done(((bf16[64,16,256]{2,0,1:T(8,128)(2,1)}), bf16[64,16,256]{2,0,1:T(8,128)(2,1)S(1)}, u32[]{:S(2)}, u32[]{:S(2)}) %all-to-all-start.3) | async-done | bytes 524320 | tf_op jit(solution)/shard_map/all_to_all | solution.py:69
  132.9 2.2 fusion.23
  136.0 0.8 copy-done.2
  138.7 2.2 collective-permute-start.3
  142.0 0.9 multiply_reduce_fusion.3
  142.9 0.6 fusion.3
  144.4 1.5 multiply_convert_fusion.1
  146.5 1.0 copy-done.10
  147.5 1.2 convolution_add_fusion.3
  148.8 0.7 pad_maximum_fusion.3
  149.5 4.6 %all-to-all-start.6 = ((bf16[16,64,128]{2,1,0:T(8,128)(2,1)}), bf16[16,64,128]{2,1,0:T(8,128)(2,1)}, u32[]{:S(2)}, u32[]{:S(2)}) async-start(bf16[16,64,128]{2,1,0:T(8,128)(2,1)} %bitcast.118), calls=%async_computation.6 | async-start | bytes 524288 | tf_op jit(solution)/shard_map/all_to_all | solution.py:130
  154.1 1.7 fusion.30
  155.8 1.0 slice.172
  156.8 4.0 %collective-permute-start.2 = (f32[512,128]{1,0:T(8,128)S(1)}, f32[512,128]{1,0:T(8,128)S(1)}, u32[]{:S(2)}, u32[]{:S(2)}) collective-permute-start(f32[512,128]{1,0:T(8,128)S(1)} %slice.172), channel_id=1, source_target_pairs={{16,0},{32,16},{48,32},{64,48},{80,64},{96,80},{112,96},{128,112},... | collective-permute-start | bytes 786440 | tf_op jit(solution)/shard_map/ppermute | solution.py:17
  161.5 1.6 fusion.14
  163.1 6.4 %collective-permute-done.2 = f32[512,128]{1,0:T(8,128)S(1)} collective-permute-done((f32[512,128]{1,0:T(8,128)S(1)}, f32[512,128]{1,0:T(8,128)S(1)}, u32[]{:S(2)}, u32[]{:S(2)}) %collective-permute-start.2) | collective-permute-done | bytes 262176 | tf_op jit(solution)/shard_map/ppermute | solution.py:17
  169.6 0.7 pad_maximum_fusion.2
  170.3 2.9 %all-to-all-done.6 = bf16[16,64,128]{2,1,0:T(8,128)(2,1)} async-done(((bf16[16,64,128]{2,1,0:T(8,128)(2,1)}), bf16[16,64,128]{2,1,0:T(8,128)(2,1)}, u32[]{:S(2)}, u32[]{:S(2)}) %all-to-all-start.6) | async-done | bytes 262176 | tf_op jit(solution)/shard_map/all_to_all | solution.py:130
  173.2 9.1 %all-to-all-start.5 = ((bf16[16,64,128]{2,1,0:T(8,128)(2,1)}), bf16[16,64,128]{2,1,0:T(8,128)(2,1)S(1)}, u32[]{:S(2)}, u32[]{:S(2)}) async-start(bf16[16,64,128]{2,1,0:T(8,128)(2,1)} %bitcast.20), calls=%async_computation.5 | async-start | bytes 524288 | tf_op jit(solution)/shard_map/all_to_all | solution.py:129
  182.4 1.7 convolution_convert_fusion.6
  185.2 1.0 copy.58
  186.2 17.6 %all-to-all-done.5 = bf16[16,64,128]{2,1,0:T(8,128)(2,1)S(1)} async-done(((bf16[16,64,128]{2,1,0:T(8,128)(2,1)}), bf16[16,64,128]{2,1,0:T(8,128)(2,1)S(1)}, u32[]{:S(2)}, u32[]{:S(2)}) %all-to-all-start.5) | async-done | bytes 262176 | tf_op jit(solution)/shard_map/all_to_all | solution.py:129
  203.9 3.8 %all-to-all-start.4 = ((bf16[16,64,256]{2,1,0:T(8,128)(2,1)}), bf16[16,64,256]{2,1,0:T(8,128)(2,1)S(1)}, u32[]{:S(2)}, u32[]{:S(2)}) async-start(bf16[16,64,256]{2,1,0:T(8,128)(2,1)} %bitcast.18), calls=%async_computation.4 | async-start | bytes 1048576 | tf_op jit(solution)/shard_map/all_to_all | solution.py:128
  207.7 1.7 copy_bitcast_fusion.2
  209.4 0.7 copy_bitcast_fusion.3
  210.1 30.8 %all-to-all-done.4 = bf16[16,64,256]{2,1,0:T(8,128)(2,1)S(1)} async-done(((bf16[16,64,256]{2,1,0:T(8,128)(2,1)}), bf16[16,64,256]{2,1,0:T(8,128)(2,1)S(1)}, u32[]{:S(2)}, u32[]{:S(2)}) %all-to-all-start.4) | async-done | bytes 524320 | tf_op jit(solution)/shard_map/all_to_all | solution.py:128
  240.9 0.8 copy.70
  (106 shorter events, 8.5 us)
Async XLA Ops:
  0.6 1.0 copy-start
  0.6 42.3 %copy-start.16 = (bf16[64,4096]{1,0:T(8,128)(2,1)S(1)}, bf16[64,4096]{1,0:T(8,128)(2,1)}, u32[]{:S(2)}) copy-start(bf16[64,4096]{1,0:T(8,128)(2,1)} %param.13) | copy-start | bytes 1572868
  0.7 67.1 %copy-start.24 = (s32[32]{0:T(128)S(1)}, s32[32]{0:T(128)}, u32[]{:S(2)}) copy-start(s32[32]{0:T(128)} %param.17) | copy-start | bytes 388
  2.4 68.8 %copy-start.17 = (bf16[64,4096]{1,0:T(8,128)(2,1)S(1)}, bf16[64,4096]{1,0:T(8,128)(2,1)}, u32[]{:S(2)}) copy-start(bf16[64,4096]{1,0:T(8,128)(2,1)} %param.16) | copy-start | bytes 1572868
  2.4 36.2 %all-to-all-start = ((bf16[64,16,128]{2,0,1:T(8,128)(2,1)}), bf16[64,16,128]{2,0,1:T(8,128)(2,1)S(1)}, u32[]{:S(2)}, u32[]{:S(2)}) async-start(bf16[64,16,128]{2,0,1:T(8,128)(2,1)} %copy_bitcast_fusion.5), calls=%async_computation | async-start | bytes 524288 | tf_op jit(solution)/shard_map/all_to_all | solution.py:67
  38.6 25.2 %all-to-all-start.2 = ((bf16[64,16,128]{2,0,1:T(8,128)(2,1)}), bf16[64,16,128]{2,0,1:T(8,128)(2,1)S(1)}, u32[]{:S(2)}, u32[]{:S(2)}) async-start(bf16[64,16,128]{2,0,1:T(8,128)(2,1)} %copy_bitcast_fusion.4), calls=%async_computation.2 | async-start | bytes 524288 | tf_op jit(solution)/shard_map/all_to_all | solution.py:68
  63.8 34.5 %all-to-all-start.1 = ((bf16[64,16,256]{2,0,1:T(8,128)(2,1)}), bf16[64,16,256]{2,0,1:T(8,128)(2,1)S(1)}, u32[]{:S(2)}, u32[]{:S(2)}) async-start(bf16[64,16,256]{2,0,1:T(8,128)(2,1)} %bitcast.81), calls=%async_computation.1 | async-start | bytes 1048576 | tf_op jit(solution)/shard_map/all_to_all | solution.py:66
  67.7 38.9 %copy-start.19 = (s32[512]{0:T(512)}, s32[512]{0:T(512)S(1)}, u32[]{:S(2)}) copy-start(s32[512]{0:T(512)S(1)} %iota_add_fusion.2) | copy-start | bytes 6148
  68.0 38.7 %copy-start.25 = (s32[512]{0:T(512)}, s32[512]{0:T(512)S(1)}, u32[]{:S(2)}) copy-start(s32[512]{0:T(512)S(1)} %broadcast_add_fusion.2) | copy-start | bytes 6148
  68.0 38.6 %copy-start.22 = (s32[1024]{0:T(1024)}, s32[1024]{0:T(1024)S(1)}, u32[]{:S(2)}) copy-start(s32[1024]{0:T(1024)S(1)} %broadcast_add_fusion) | copy-start | bytes 12292
  68.0 34.2 %collective-permute-start = (bf16[512,128]{1,0:T(8,128)(2,1)S(1)}, bf16[512,128]{1,0:T(8,128)(2,1)S(1)}, u32[]{:S(2)}, u32[]{:S(2)}) collective-permute-start(bf16[512,128]{1,0:T(8,128)(2,1)S(1)} %bitcast.122), channel_id=1, source_target_pairs={{0,16},{16,32},{32,48},{48,64},{64,80},{80,96},{96,112},{112,128},... | collective-permute-start | bytes 393224 | tf_op jit(solution)/shard_map/ppermute | solution.py:17
  71.2 35.5 %copy-start.31 = (pred[512]{0:T(512)(128)(4,1)}, pred[512]{0:T(512)(128)(4,1)S(1)}, u32[]{:S(2)}) copy-start(pred[512]{0:T(512)(128)(4,1)S(1)} %broadcast_compare_fusion.2) | copy-start | bytes 1540
  72.1 34.6 %copy-start.29 = (pred[1024]{0:T(1024)(128)(4,1)}, pred[1024]{0:T(1024)(128)(4,1)S(1)}, u32[]{:S(2)}) copy-start(pred[1024]{0:T(1024)(128)(4,1)S(1)} %broadcast_compare_fusion) | copy-start | bytes 3076
  72.7 68.2 %collective-permute-start.1 = (bf16[512,128]{1,0:T(8,128)(2,1)}, bf16[512,128]{1,0:T(8,128)(2,1)S(1)}, u32[]{:S(2)}, u32[]{:S(2)}) collective-permute-start(bf16[512,128]{1,0:T(8,128)(2,1)} %bitcast.7), channel_id=1, source_target_pairs={{0,16},{16,32},{32,48},{48,64},{64,80},{80,96},{96,112},{112,128},... | collective-permute-start | bytes 393224 | tf_op jit(solution)/shard_map/ppermute | solution.py:17
  98.4 8.3 %copy-start.14 = (bf16[64,16,256]{2,0,1:T(8,128)(2,1)}, bf16[64,16,256]{2,0,1:T(8,128)(2,1)S(1)}, u32[]{:S(2)}) copy-start(bf16[64,16,256]{2,0,1:T(8,128)(2,1)S(1)} %all-to-all-done.1) | copy-start | bytes 1572868
  98.4 34.6 %all-to-all-start.3 = ((bf16[64,16,256]{2,0,1:T(8,128)(2,1)}), bf16[64,16,256]{2,0,1:T(8,128)(2,1)S(1)}, u32[]{:S(2)}, u32[]{:S(2)}) async-start(bf16[64,16,256]{2,0,1:T(8,128)(2,1)} %bitcast.80), calls=%async_computation.3 | async-start | bytes 1048576 | tf_op jit(solution)/shard_map/all_to_all | solution.py:69
  102.2 2.9 %copy-start.27 = (bf16[512,128]{1,0:T(8,128)(2,1)}, bf16[512,128]{1,0:T(8,128)(2,1)S(1)}, u32[]{:S(2)}) copy-start(bf16[512,128]{1,0:T(8,128)(2,1)S(1)} %collective-permute-done) | copy-start | bytes 393220
  103.4 1.3 copy-start.3
  106.2 1.6 copy-start.1
  107.8 1.3 copy-start.5
  107.8 1.3 copy-start.20
  107.8 1.3 copy-start.23
  107.9 1.3 copy-start.26
  107.9 1.3 copy-start.30
  107.9 1.3 copy-start.32
  132.9 2.2 copy-start.6
  132.9 2.7 %copy-start.21 = (f32[512]{0:T(512)S(1)}, f32[512]{0:T(512)}, u32[]{:S(2)}) copy-start(f32[512]{0:T(512)} %get-tuple-element.65) | copy-start | bytes 6148
  135.2 1.6 copy-start.2
  138.7 2.8 %copy-start.4 = (f32[512,1024]{0,1:T(8,128)S(1)}, f32[512,1024]{0,1:T(8,128)}, u32[]{:S(2)}) copy-start(f32[512,1024]{0,1:T(8,128)} %copy-done.3) | copy-start | bytes 6291460
  138.7 10.1 %collective-permute-start.3 = (f32[512,128]{1,0:T(8,128)S(1)}, f32[512,128]{1,0:T(8,128)S(1)}, u32[]{:S(2)}, u32[]{:S(2)}) collective-permute-start(f32[512,128]{1,0:T(8,128)S(1)} %slice.175), channel_id=1, source_target_pairs={{16,0},{32,16},{48,32},{64,48},{80,64},{96,80},{112,96},{128,112},... | collective-permute-start | bytes 786440 | tf_op jit(solution)/shard_map/ppermute | solution.py:17
  142.9 1.0 copy-start.15
  144.0 2.0 copy-start.12
  146.5 1.0 copy-start.10
  148.8 12.1 %copy-start.18 = (f32[512]{0:T(512)S(1)}, f32[512]{0:T(512)}, u32[]{:S(2)}) copy-start(f32[512]{0:T(512)} %get-tuple-element.54) | copy-start | bytes 6148
  149.5 23.7 %all-to-all-start.6 = ((bf16[16,64,128]{2,1,0:T(8,128)(2,1)}), bf16[16,64,128]{2,1,0:T(8,128)(2,1)}, u32[]{:S(2)}, u32[]{:S(2)}) async-start(bf16[16,64,128]{2,1,0:T(8,128)(2,1)} %bitcast.118), calls=%async_computation.6 | async-start | bytes 524288 | tf_op jit(solution)/shard_map/all_to_all | solution.py:130
  155.8 5.7 %copy-start.13 = (f32[1024,128]{1,0:T(8,128)S(1)}, f32[1024,128]{1,0:T(8,128)}, u32[]{:S(2)}) copy-start(f32[1024,128]{1,0:T(8,128)} %convolution_add_fusion.3) | copy-start | bytes 1572868
  156.8 12.7 %collective-permute-start.2 = (f32[512,128]{1,0:T(8,128)S(1)}, f32[512,128]{1,0:T(8,128)S(1)}, u32[]{:S(2)}, u32[]{:S(2)}) collective-permute-start(f32[512,128]{1,0:T(8,128)S(1)} %slice.172), channel_id=1, source_target_pairs={{16,0},{32,16},{48,32},{64,48},{80,64},{96,80},{112,96},{128,112},... | collective-permute-start | bytes 786440 | tf_op jit(solution)/shard_map/ppermute | solution.py:17
  161.5 8.1 %copy-start.8 = (bf16[512,1024]{0,1:T(8,128)(2,1)}, bf16[512,1024]{0,1:T(8,128)(2,1)S(1)}, u32[]{:S(2)}) copy-start(bf16[512,1024]{0,1:T(8,128)(2,1)S(1)} %multiply_convert_fusion) | copy-start | bytes 3145732
  161.5 20.9 %copy-start.28 = (bf16[512,128]{1,0:T(8,128)(2,1)S(1)}, bf16[512,128]{1,0:T(8,128)(2,1)}, u32[]{:S(2)}) copy-start(bf16[512,128]{1,0:T(8,128)(2,1)} %copy-done.27) | copy-start | bytes 393220
  163.1 21.0 %copy-start.11 = (bf16[512,1024]{0,1:T(8,128)(2,1)S(1)}, bf16[512,1024]{0,1:T(8,128)(2,1)}, u32[]{:S(2)}) copy-start(bf16[512,1024]{0,1:T(8,128)(2,1)} %copy-done.10) | copy-start | bytes 3145732
  169.6 14.8 %copy-start.7 = (bf16[512,1024]{0,1:T(8,128)(2,1)S(1)}, bf16[512,1024]{0,1:T(8,128)(2,1)}, u32[]{:S(2)}) copy-start(bf16[512,1024]{0,1:T(8,128)(2,1)} %multiply_convert_fusion.1) | copy-start | bytes 3145732
  173.2 30.6 %all-to-all-start.5 = ((bf16[16,64,128]{2,1,0:T(8,128)(2,1)}), bf16[16,64,128]{2,1,0:T(8,128)(2,1)S(1)}, u32[]{:S(2)}, u32[]{:S(2)}) async-start(bf16[16,64,128]{2,1,0:T(8,128)(2,1)} %bitcast.20), calls=%async_computation.5 | async-start | bytes 524288 | tf_op jit(solution)/shard_map/all_to_all | solution.py:129
  182.4 2.4 copy-start.9
  203.9 37.0 %all-to-all-start.4 = ((bf16[16,64,256]{2,1,0:T(8,128)(2,1)}), bf16[16,64,256]{2,1,0:T(8,128)(2,1)S(1)}, u32[]{:S(2)}, u32[]{:S(2)}) async-start(bf16[16,64,256]{2,1,0:T(8,128)(2,1)} %bitcast.18), calls=%async_computation.4 | async-start | bytes 1048576 | tf_op jit(solution)/shard_map/all_to_all | solution.py:128
where the time goes:
time: 243 us; the launch traced here: 242 us
  waiting for transfers between devices  144 us (59%)
  starting transfers between devices  53.9 us (22%)
  matrix products  22.4 us (9%)
  local copies, waits for them, and re-layouts  15.7 us (6%)
  other arithmetic  4.23 us (2%)
    all_to_all x1, waiting for transfers between devices, shards(): lax.all_to_all(dquery_local, 'head', split_axis=0, concat_axis=1, tiled=T...  30.8 us
    all_to_all x1, waiting for transfers between devices, shards(): lax.all_to_all(keys, 'head', split_axis=1, concat_axis=0, tiled=True)  22.6 us
    all_to_all x1, waiting for transfers between devices, shards(): lax.all_to_all(queries, 'head', split_axis=1, concat_axis=0, tiled=True)  22.5 us
    all_to_all x1, waiting for transfers between devices, shards(): lax.all_to_all(dout, 'head', split_axis=1, concat_axis=0, tiled=True)  21.1 us
    all_to_all x1, waiting for transfers between devices, shards(): lax.all_to_all(values, 'head', split_axis=1, concat_axis=0, tiled=True)  20.1 us
    all_to_all x1, waiting for transfers between devices, shards(): lax.all_to_all(dkey_local, 'head', split_axis=0, concat_axis=1, tiled=True)  17.6 us
    ppermute x4, starting transfers between devices, passed_along(): return lax.ppermute(x, axis, pairs)  12.5 us
    all_to_all x1, starting transfers between devices, shards(): lax.all_to_all(keys, 'head', split_axis=1, concat_axis=0, tiled=True)  11.9 us
  transfers between devices with their start and end apart: 11, of which 8 were waited for; matrix products, arithmetic and copies ran while one was open for 14% of the time, Pallas kernels for 0%

commit v1 on v0

v1 whole, which is shorter than its diff:
```python
import jax
import jax.numpy as jnp
from jax import lax
from jax.experimental import pallas as pl
from jax.experimental.pallas import tpu as pltpu
from jax.sharding import PartitionSpec as P

MESH = pl.DeviceIdType.MESH
HEAD = 128
ROWS = 64
WINDOW = 512
BLOCK = 1024
SPAN = WINDOW + BLOCK
TILE = 128
REACH = TILE + WINDOW
KV_HEADS = 16
Q_HEADS = 32
GROUPS = 8
PIECES = 2
SCALE = 168.0 ** -0.5
TO_EXP2 = SCALE * 1.4426950408889634
NEGATIVE = -1.0e30


def kernel(
    q_hbm, k_hbm, v_hbm, g_hbm, doc_ref, dq_ref, dk_ref, dv_ref,
    q_in, k_in, v_in, g_in, kvs, qgs, kvx, qgx, lo_ref, acc, hs, hr, rs, dqs, rr, dqr,
    load_sem, kv_send, kv_recv, qg_send, qg_recv, x_send, x_recv, halo_send, halo_recv,
    back_send, back_recv, r_send, r_recv, dq_send, dq_recv,
):
    seq, head = lax.axis_index("seq"), lax.axis_index("head")
    zl, x = seq // 4, seq % 4
    y, zh, c = head // 4, (head // 2) % 2, head % 2
    other = 1 - zh
    group = y * 2 + c
    rng = (x + 4 - y) % 4
    first = (rng == 0) & (zl == 0)
    last = (rng == 3) & (zl == 7)

    def place(px, py, pzh, pzl, pc):
        return (pzl * 4 + px, py * 4 + pzh * 2 + pc)

    def worker(g, side):
        gy = g // 2
        return place((x + gy) % 4, gy, side, zl, g % 2)

    def owner(o, side):
        return place(rng, o // 2, side, zl, o % 2)

    before = place((x + 3) % 4, y, zh, zl - (rng == 0).astype(jnp.int32), c)
    after = place((x + 1) % 4, y, zh, zl + (rng == 3).astype(jnp.int32), c)

    def is_me(dev):
        return (dev[0] == seq) & (dev[1] == head)

    def remote(src, dst, ssem, rsem, dev):
        return pltpu.make_async_remote_copy(
            src_ref=src, dst_ref=dst, send_sem=ssem, recv_sem=rsem, device_id=dev, device_id_type=MESH
        )

    def send(src, dst, ssem, rsem, dev):
        me = is_me(dev)

        @pl.when(me)
        def _():
            pltpu.make_async_copy(src, dst, rsem).start()

        @pl.when(jnp.logical_not(me))
        def _():
            remote(src, dst, ssem, rsem, dev).start()

    def sent(src, dst, ssem, rsem, dev):
        @pl.when(jnp.logical_not(is_me(dev)))
        def _():
            remote(src, dst, ssem, rsem, dev).wait_send()

    def arrived(dst, rsem):
        pltpu.make_async_copy(dst, dst, rsem).wait()

    def each(count, body):
        def step(n, carry):
            body(n)
            return carry

        lax.fori_loop(0, count, step, 0)

    loads = [
        pltpu.make_async_copy(src, dst, load_sem.at[n])
        for n, (src, dst) in enumerate(((k_hbm, k_in), (v_hbm, v_in), (q_hbm, q_in), (g_hbm, g_in)))
    ]
    for load in loads:
        load.start()

    barrier = pltpu.get_barrier_semaphore()

    def greet(dev):
        pl.semaphore_signal(barrier, inc=1, device_id=dev, device_id_type=MESH)

    def greet_group(n):
        g = (n + group) % GROUPS
        greet(worker(g, other))
        greet(owner(g, other))

        @pl.when(jnp.logical_not(is_me(worker(g, zh))))
        def _():
            greet(worker(g, zh))

        @pl.when(jnp.logical_not(is_me(owner(g, zh))))
        def _():
            greet(owner(g, zh))

    each(GROUPS, greet_group)

    @pl.when(jnp.logical_not(first))
    def _():
        greet(before)

    @pl.when(jnp.logical_not(last))
    def _():
        greet(after)

    loads[0].wait()
    loads[1].wait()
    for h in range(KV_HEADS):
        kvs[h, 0] = k_in[:, h * HEAD : (h + 1) * HEAD]
        kvs[h, 1] = v_in[:, h * HEAD : (h + 1) * HEAD]

    own = jnp.where(y == 0, 2, 0)
    pl.semaphore_wait(
        barrier, 4 * GROUPS + 2 - own - first.astype(jnp.int32) - last.astype(jnp.int32)
    )

    token = pl.multiple_of(WINDOW + y * 256 + zh * 128 + c * ROWS, ROWS)
    query = pl.multiple_of(y * 128 + c * ROWS, ROWS)

    def cross(i, n):
        g = (n + group) % GROUPS
        return remote(
            kvs.at[g * PIECES + i], kvx.at[i, :, pl.ds(token, ROWS), :],
            x_send.at[i, n], x_recv.at[i, group], worker(g, other),
        )

    each(GROUPS, lambda n: cross(0, n).start())

    def kv_args(n):
        g = (n + group) % GROUPS
        return (
            kvs.at[pl.ds(g * PIECES, PIECES)], kvx.at[:, :, pl.ds(token, ROWS), :],
            kv_send.at[n], kv_recv.at[group], worker(g, zh),
        )

    each(GROUPS, lambda n: send(*kv_args(n)))

    loads[2].wait()
    loads[3].wait()
    for h in range(Q_HEADS):
        qgs[h, 0] = q_in[:, h * HEAD : (h + 1) * HEAD]
        qgs[h, 1] = g_in[:, h * HEAD : (h + 1) * HEAD]

    def qg_args(n):
        g = (n + group) % GROUPS
        return (
            qgs.at[pl.ds(g * 4, 4)], qgx.at[:, :, pl.ds(query, ROWS), :],
            qg_send.at[n], qg_recv.at[group], worker(g, zh),
        )

    each(GROUPS, lambda n: send(*qg_args(n)))

    base = (zl * 4 + rng) * BLOCK
    lane = lax.broadcasted_iota(jnp.int32, (8, 2 * TILE), 1) % TILE
    for j in range(4):
        tile_at = base + (2 * j + zh) * TILE
        position = tile_at + lane
        start = jnp.zeros((8, 2 * TILE), jnp.int32)
        for d in range(32):
            start = jnp.where(doc_ref[d] <= position, jnp.maximum(start, doc_ref[d]), start)
        lo_ref[j] = jnp.maximum(lane + 1, start - (tile_at - WINDOW))

    @pl.when(first)
    def _():
        kvx[:, :, :WINDOW, :] = jnp.zeros((PIECES, 2, WINDOW, HEAD), jnp.bfloat16)

    @pl.when(last)
    def _():
        hr[...] = jnp.zeros(hr.shape, jnp.bfloat16)

    def second(n):
        cross(0, n).wait_send()
        cross(1, n).start()

    each(GROUPS, second)

    def tile(i, j):
        w = pl.multiple_of((2 * j + zh) * TILE, TILE)
        keys = kvx[i, 0, pl.ds(w, REACH), :]
        values = kvx[i, 1, pl.ds(w, REACH), :]
        at = slice(j * TILE, (j + 1) * TILE)
        qt = qgx[2 * i : 2 * i + 2, 0, at, :].reshape(2 * TILE, HEAD)
        gt = qgx[2 * i : 2 * i + 2, 1, at, :].reshape(2 * TILE, HEAD)
        rows = (((1,), (1,)), ((), ()))
        raw = lax.dot_general(keys, qt, rows, preferred_element_type=jnp.float32)
        key_at = lax.broadcasted_iota(jnp.int32, (REACH, 2 * TILE), 0)
        lane_at = lax.broadcasted_iota(jnp.int32, (REACH, 2 * TILE), 1) % TILE
        allowed = (key_at >= lo_ref[j, 0:1, :]) & (key_at <= lane_at + WINDOW)
        raw = jnp.where(allowed, raw, NEGATIVE)
        peak = jnp.max(raw, axis=0, keepdims=True)
        weight = jnp.exp2((raw - peak) * TO_EXP2)
        probs = weight * (1.0 / jnp.sum(weight, axis=0, keepdims=True))
        dprobs = lax.dot_general(values, gt, rows, preferred_element_type=jnp.float32)
        delta = jnp.sum(probs * dprobs, axis=0, keepdims=True)
        dscores = (probs * (dprobs - delta)).astype(jnp.bfloat16)
        acc[0, pl.ds(w, REACH), :] += jnp.dot(dscores, qt, preferred_element_type=jnp.float32)
        acc[1, pl.ds(w, REACH), :] += jnp.dot(
            probs.astype(jnp.bfloat16), gt, preferred_element_type=jnp.float32
        )
        dq = lax.dot_general(
            dscores, keys, (((0,), (0,)), ((), ())), preferred_element_type=jnp.float32
        )
        dq = (dq * SCALE).astype(jnp.bfloat16)
        for core in range(2):
            for member in range(2):
                row = member * TILE + core * ROWS
                dqs[i, 2 * j + core, member] = dq[row : row + ROWS]

    def result_args(i, side, o):
        return (
            rs.at[i, side, o], rr.at[zh, group * PIECES + i],
            r_send.at[i, side, o], r_recv.at[zh, group * PIECES + i], owner(o, side),
        )

    def dq_args(i, o):
        return (
            dqs.at[i, o], dqr.at[pl.ds(group * 4 + 2 * i, 2)],
            dq_send.at[i, o], dq_recv.at[group * PIECES + i], owner(o, zh),
        )

    def results(i, half):
        for side in range(2):
            for o in range(4 * half, 4 * half + 4):
                at = WINDOW + (o // 2) * 256 + side * 128 + (o % 2) * ROWS
                for kind in range(2):
                    part = acc[kind, at : at + ROWS, :]
                    if half:
                        part = part + hr[i, kind, at - BLOCK : at - BLOCK + ROWS, :].astype(jnp.float32)
                    if kind == 0:
                        part = part * SCALE
                    rs[i, side, o, kind] = part.astype(jnp.bfloat16)
        each(4, lambda n: remote(*result_args(i, other, 4 * half + n)).start())
        each(4, lambda n: send(*result_args(i, zh, 4 * half + n)))

    for i in range(PIECES):
        if i == 0:
            def ready(n):
                arrived(kvx.at[:, :, pl.ds(0, ROWS), :], kv_recv.at[n])
                arrived(qgx.at[:, :, pl.ds(0, ROWS), :], qg_recv.at[n])

            each(GROUPS, ready)
        each(GROUPS, lambda n: arrived(kvx.at[i, :, pl.ds(0, ROWS), :], x_recv.at[i, n]))
        halo = remote(
            kvx.at[i, :, pl.ds(BLOCK, WINDOW), :], kvx.at[i, :, pl.ds(0, WINDOW), :],
            halo_send.at[i], halo_recv.at[i], after,
        )
        back = remote(hs.at[i], hr.at[i], back_send.at[i], back_recv.at[i], before)

        @pl.when(jnp.logical_not(last))
        def _():
            halo.start()

        acc[...] = jnp.zeros(acc.shape, jnp.float32)
        tile(i, 3)
        tile(i, 2)

        @pl.when(jnp.logical_not(first))
        def _():
            arrived(kvx.at[i, :, pl.ds(0, WINDOW), :], halo_recv.at[i])

        tile(i, 1)
        tile(i, 0)

        hs[i] = acc[:, :WINDOW, :].astype(jnp.bfloat16)

        @pl.when(jnp.logical_not(first))
        def _():
            back.start()

        results(i, 0)
        each(GROUPS, lambda n: send(*dq_args(i, n)))

        @pl.when(jnp.logical_not(last))
        def _():
            arrived(hr.at[i], back_recv.at[i])

        results(i, 1)

    for i in range(PIECES):
        for g in range(GROUPS):
            h = g * PIECES + i
            arrived(dqr.at[pl.ds(2 * h, 2)], dq_recv.at[h])
            for member in range(2):
                at = (2 * h + member) * HEAD
                dq_ref[:, at : at + HEAD] = dqr[2 * h + member]
            arrived(rr.at[0, h], r_recv.at[0, h])
            arrived(rr.at[1, h], r_recv.at[1, h])
            total = (rr[0, h].astype(jnp.float32) + rr[1, h].astype(jnp.float32)).astype(jnp.bfloat16)
            dk_ref[:, h * HEAD : (h + 1) * HEAD] = total[0]
            dv_ref[:, h * HEAD : (h + 1) * HEAD] = total[1]

    def finish(n):
        sent(*kv_args(n))
        sent(*qg_args(n))
        cross(1, n).wait_send()
        for i in range(PIECES):
            remote(*result_args(i, other, n)).wait_send()
            sent(*result_args(i, zh, n))
            sent(*dq_args(i, n))

    each(GROUPS, finish)
    for i in range(PIECES):
        @pl.when(jnp.logical_not(last))
        def _():
            remote(
                kvx.at[i, :, pl.ds(BLOCK, WINDOW), :], kvx.at[i, :, pl.ds(0, WINDOW), :],
                halo_send.at[i], halo_recv.at[i], after,
            ).wait_send()

        @pl.when(jnp.logical_not(first))
        def _():
            remote(hs.at[i], hr.at[i], back_send.at[i], back_recv.at[i], before).wait_send()


def shards(queries, keys, values, dout, doc_starts):
    bf16, f32 = jnp.bfloat16, jnp.float32
    dma = pltpu.SemaphoreType.DMA
    return tuple(
        pl.pallas_call(
            kernel,
            out_shape=(
                jax.ShapeDtypeStruct(queries.shape, bf16),
                jax.ShapeDtypeStruct(keys.shape, bf16),
                jax.ShapeDtypeStruct(values.shape, bf16),
            ),
            in_specs=[pl.BlockSpec(memory_space=pl.ANY)] * 4 + [pl.BlockSpec(memory_space=pltpu.SMEM)],
            out_specs=(pl.BlockSpec(memory_space=pltpu.VMEM),) * 3,
            scratch_shapes=[
                pltpu.VMEM((ROWS, Q_HEADS * HEAD), bf16),
                pltpu.VMEM((ROWS, KV_HEADS * HEAD), bf16),
                pltpu.VMEM((ROWS, KV_HEADS * HEAD), bf16),
                pltpu.VMEM((ROWS, Q_HEADS * HEAD), bf16),
                pltpu.VMEM((KV_HEADS, 2, ROWS, HEAD), bf16),
                pltpu.VMEM((Q_HEADS, 2, ROWS, HEAD), bf16),
                pltpu.VMEM((PIECES, 2, SPAN, HEAD), bf16),
                pltpu.VMEM((4, 2, WINDOW, HEAD), bf16),
                pltpu.VMEM((4, 8, 2 * TILE), jnp.int32),
                pltpu.VMEM((2, SPAN, HEAD), f32),
                pltpu.VMEM((PIECES, 2, WINDOW, HEAD), bf16),
                pltpu.VMEM((PIECES, 2, WINDOW, HEAD), bf16),
                pltpu.VMEM((PIECES, 2, GROUPS, 2, ROWS, HEAD), bf16),
                pltpu.VMEM((PIECES, GROUPS, 2, ROWS, HEAD), bf16),
                pltpu.VMEM((2, KV_HEADS, 2, ROWS, HEAD), bf16),
                pltpu.VMEM((Q_HEADS, ROWS, HEAD), bf16),
                dma((4,)),
                dma((GROUPS,)), dma((GROUPS,)),
                dma((GROUPS,)), dma((GROUPS,)),
                dma((PIECES, GROUPS)), dma((PIECES, GROUPS)),
                dma((PIECES,)), dma((PIECES,)),
                dma((PIECES,)), dma((PIECES,)),
                dma((PIECES, 2, GROUPS)), dma((2, KV_HEADS)),
                dma((PIECES, GROUPS)), dma((KV_HEADS,)),
            ],
            compiler_params=pltpu.CompilerParams(
                collective_id=0, has_side_effects=True, vmem_limit_bytes=40 * 1024 * 1024
            ),
        )(queries, keys, values, dout, doc_starts)
    )


def solution(mesh):
    rows = P(("seq", "head"), None)
    return jax.shard_map(
        shards,
        mesh=mesh,
        in_specs=(rows, rows, rows, rows, P()),
        out_specs=(rows, rows, rows),
        check_vma=False,
    )
```

time: 243 us -> 168 us (0.69)
  the two profiles are of different devices: /device:TPU:193 before, /device:TPU:63 now
where the time goes in v1:
time: 168 us; the launch traced here: 167 us
  Pallas kernels  160 us (95%)
  local copies, waits for them, and re-layouts  6.83 us (4%)
    pallas_call x1, Pallas kernels, shards(): pl.pallas_call(kernel, out_shape=(jax.ShapeDtypeStruct(queries.shape, bf1...  160 us
    unnamed x13, local copies, waits for them, and re-layouts  6.83 us

profile of v1, /device:TPU:63, one launch (start us, length us, event | category | flops | bytes accessed | tf_op | source)
XLA Modules:
  0.0 167.3 jit_solution(8125512011847288471)
XLA Ops:
  0.6 0.0 copy-start
  0.6 1.0 copy-done
  1.7 0.0 copy-start.1
  1.7 1.0 copy-done.1
  2.7 0.0 copy-start.2
  2.7 0.9 copy-done.2
  3.7 0.0 copy-start.3
  3.7 0.9 copy-done.3
  4.6 0.0 copy-start.4
  4.6 0.7 copy-done.4
  5.3 159.8 %shard_map.76 = (bf16[64,4096]{1,0:T(8,128)(2,1)S(1)}, bf16[64,2048]{1,0:T(8,128)(2,1)S(1)}, bf16[64,2048]{1,0:T(8,128)(2,1)S(1)}) custom-call(bf16[64,4096]{1,0:T(8,128)(2,1)S(1)} %copy-done, bf16[64,2048]{1,0:T(8,128)(2,1)S(1)} %copy-done.2, bf16[64,2048]{1,0:T(8,128)(2,1)S(1)} %copy-done.3, bf16[64,4096]{1,0:T(8,128)(2,1)S(1)} %copy-done.1, s32[32]{0:T(128)S(1)} %copy-done.4), custom_call_target="tpu_custom_call" | custom-call | tf_op jit(solution)/shard_map/pallas_call | solution.py:335
  165.1 0.8 copy.11
  165.9 0.7 copy.12
  166.6 0.7 copy.13
Async XLA Ops:
  0.6 1.0 copy-start
  1.7 1.0 copy-start.1
  2.7 0.9 copy-start.2
  3.7 0.9 copy-start.3
  4.6 0.7 copy-start.4

commit v2 on v1

v2 whole, which is shorter than its diff:
```python
import jax
import jax.numpy as jnp
from jax import lax
from jax.experimental import pallas as pl
from jax.experimental.pallas import tpu as pltpu
from jax.sharding import PartitionSpec as P

MESH = pl.DeviceIdType.MESH
HEAD = 128
ROWS = 64
WINDOW = 512
BLOCK = 1024
SPAN = WINDOW + BLOCK
TILE = 128
REACH = TILE + WINDOW
KV_HEADS = 16
Q_HEADS = 32
GROUPS = 8
PIECES = 2
SCALE = 168.0 ** -0.5
TO_EXP2 = SCALE * 1.4426950408889634
NEGATIVE = -1.0e30


def kernel(
    q_hbm, k_hbm, v_hbm, g_hbm, doc_ref, dq_ref, dk_ref, dv_ref,
    q_in, k_in, v_in, g_in, kvs, qgs, kvx, qgx, lo_ref, acc, hs, hr, rs, dqs, rr, dqr,
    load_sem, kv_send, kv_recv, qg_send, qg_recv, x_send, x_recv, halo_send, halo_recv,
    back_send, back_recv, r_send, r_recv, dq_send, dq_recv,
):
    seq, head = lax.axis_index("seq"), lax.axis_index("head")
    zl, x = seq >> 2, seq & 3
    y, zh, c = head >> 2, (head >> 1) & 1, head & 1
    other = 1 - zh
    group = y * 2 + c
    rngs = [(x + 8 - 2 * i - c) & 3 for i in range(PIECES)]
    firsts = [(rng == 0) & (zl == 0) for rng in rngs]
    lasts = [(rng == 3) & (zl == 7) for rng in rngs]
    held = rngs[0] == 3

    def place(px, py, pzh, pzl, pc):
        return (pzl * 4 + px, py * 4 + pzh * 2 + pc)

    def worker(i, g, side):
        gc = g & 1
        return place((x + 2 * i + gc) & 3, g >> 1, side, zl, gc)

    def owner(i, o, side):
        return place(rngs[i], o >> 1, side, zl, o & 1)

    befores = [place((x + 3) & 3, y, zh, zl - (rng == 0).astype(jnp.int32), c) for rng in rngs]
    afters = [place((x + 1) & 3, y, zh, zl + (rng == 3).astype(jnp.int32), c) for rng in rngs]

    def is_me(dev):
        return (dev[0] == seq) & (dev[1] == head)

    def remote(src, dst, ssem, rsem, dev):
        return pltpu.make_async_remote_copy(
            src_ref=src, dst_ref=dst, send_sem=ssem, recv_sem=rsem, device_id=dev, device_id_type=MESH
        )

    def send(src, dst, ssem, rsem, dev):
        me = is_me(dev)

        @pl.when(me)
        def _():
            pltpu.make_async_copy(src, dst, rsem).start()

        @pl.when(jnp.logical_not(me))
        def _():
            remote(src, dst, ssem, rsem, dev).start()

    def sent(src, dst, ssem, rsem, dev):
        @pl.when(jnp.logical_not(is_me(dev)))
        def _():
            remote(src, dst, ssem, rsem, dev).wait_send()

    def arrived(dst, rsem):
        pltpu.make_async_copy(dst, dst, rsem).wait()

    def each(count, body):
        def step(n, carry):
            body(n)
            return carry

        lax.fori_loop(0, count, step, 0)

    loads = [
        pltpu.make_async_copy(src, dst, load_sem.at[n])
        for n, (src, dst) in enumerate(((k_hbm, k_in), (v_hbm, v_in), (q_hbm, q_in), (g_hbm, g_in)))
    ]
    for load in loads:
        load.start()

    barrier = pltpu.get_barrier_semaphore()

    def greet(dev):
        pl.semaphore_signal(barrier, inc=1, device_id=dev, device_id_type=MESH)

    def greet_plane(n):
        gx, gy, gc = ((n >> 3) + x) & 3, ((n >> 1) + y) & 3, (n + c) & 1

        @pl.when(((n & 1) == 1) | (((n >> 3) & 1) == c))
        def _():
            greet(place(gx, gy, other, zl, gc))

            @pl.when(n > 0)
            def _():
                greet(place(gx, gy, zh, zl, gc))

    each(32, greet_plane)
    greeted = 47 + c
    for i in range(PIECES):
        down = (rngs[i] == 0) & jnp.logical_not(firsts[i])
        up = (rngs[i] == 3) & jnp.logical_not(lasts[i])

        @pl.when(down)
        def _():
            greet(befores[i])

        @pl.when(up)
        def _():
            greet(afters[i])

        greeted = greeted + down.astype(jnp.int32) + up.astype(jnp.int32)

    loads[0].wait()
    loads[1].wait()
    for h in range(KV_HEADS):
        kvs[h, 0] = k_in[:, h * HEAD : (h + 1) * HEAD]
        kvs[h, 1] = v_in[:, h * HEAD : (h + 1) * HEAD]

    pl.semaphore_wait(barrier, greeted)

    token = pl.multiple_of(WINDOW + y * 256 + zh * 128 + c * ROWS, ROWS)
    query = pl.multiple_of(y * 128 + c * ROWS, ROWS)

    def cross(i, n):
        g = (n + group) & (GROUPS - 1)
        return remote(
            kvs.at[g * PIECES + i], kvx.at[i, :, pl.ds(token, ROWS), :],
            x_send.at[i, n], x_recv.at[i, group], worker(i, g, other),
        )

    def early(n):
        cross(1, n).start()

    each(GROUPS, lambda n: cross(0, n).start())

    @pl.when(jnp.logical_not(held))
    def _():
        each(GROUPS, early)

    def kv_args(i, n):
        g = (n + group) & (GROUPS - 1)
        return (
            kvs.at[g * PIECES + i], kvx.at[i, :, pl.ds(token, ROWS), :],
            kv_send.at[i, n], kv_recv.at[i, group], worker(i, g, zh),
        )

    each(GROUPS, lambda n: send(*kv_args(0, n)))

    loads[2].wait()
    loads[3].wait()
    for h in range(Q_HEADS):
        qgs[h, 0] = q_in[:, h * HEAD : (h + 1) * HEAD]
        qgs[h, 1] = g_in[:, h * HEAD : (h + 1) * HEAD]

    def qg_args(i, n):
        g = (n + group) & (GROUPS - 1)
        return (
            qgs.at[pl.ds(g * 4 + 2 * i, 2)], qgx.at[pl.ds(2 * i, 2), :, pl.ds(query, ROWS), :],
            qg_send.at[i, n], qg_recv.at[i, group], worker(i, g, zh),
        )

    each(GROUPS, lambda n: send(*qg_args(0, n)))
    each(GROUPS, lambda n: send(*kv_args(1, n)))
    each(GROUPS, lambda n: send(*qg_args(1, n)))

    lane = lax.broadcasted_iota(jnp.int32, (8, 2 * TILE), 1) % TILE
    for i in range(PIECES):
        for j in range(4):
            tile_at = (zl * 4 + rngs[i]) * BLOCK + (2 * j + zh) * TILE
            position = tile_at + lane
            start = jnp.zeros((8, 2 * TILE), jnp.int32)
            for d in range(32):
                start = jnp.where(doc_ref[d] <= position, jnp.maximum(start, doc_ref[d]), start)
            lo_ref[i, j] = jnp.maximum(lane + 1, start - (tile_at - WINDOW))

        @pl.when(firsts[i])
        def _():
            kvx[i, :, :WINDOW, :] = jnp.zeros((2, WINDOW, HEAD), jnp.bfloat16)

        @pl.when(lasts[i])
        def _():
            hr[i] = jnp.zeros((2, WINDOW, HEAD), jnp.bfloat16)

    def tile(i, j):
        w = pl.multiple_of((2 * j + zh) * TILE, TILE)
        keys = kvx[i, 0, pl.ds(w, REACH), :]
        values = kvx[i, 1, pl.ds(w, REACH), :]
        at = slice(j * TILE, (j + 1) * TILE)
        qt = qgx[2 * i : 2 * i + 2, 0, at, :].reshape(2 * TILE, HEAD)
        gt = qgx[2 * i : 2 * i + 2, 1, at, :].reshape(2 * TILE, HEAD)
        rows = (((1,), (1,)), ((), ()))
        raw = lax.dot_general(keys, qt, rows, preferred_element_type=jnp.float32)
        key_at = lax.broadcasted_iota(jnp.int32, (REACH, 2 * TILE), 0)
        lane_at = lax.broadcasted_iota(jnp.int32, (REACH, 2 * TILE), 1) % TILE
        allowed = (key_at >= lo_ref[i, j, 0:1, :]) & (key_at <= lane_at + WINDOW)
        raw = jnp.where(allowed, raw, NEGATIVE)
        peak = jnp.max(raw, axis=0, keepdims=True)
        weight = jnp.exp2((raw - peak) * TO_EXP2)
        probs = weight * (1.0 / jnp.sum(weight, axis=0, keepdims=True))
        dprobs = lax.dot_general(values, gt, rows, preferred_element_type=jnp.float32)
        delta = jnp.sum(probs * dprobs, axis=0, keepdims=True)
        dscores = (probs * (dprobs - delta)).astype(jnp.bfloat16)
        acc[i, 0, pl.ds(w, REACH), :] += jnp.dot(dscores, qt, preferred_element_type=jnp.float32)
        acc[i, 1, pl.ds(w, REACH), :] += jnp.dot(
            probs.astype(jnp.bfloat16), gt, preferred_element_type=jnp.float32
        )
        dq = lax.dot_general(
            dscores, keys, (((0,), (0,)), ((), ())), preferred_element_type=jnp.float32
        )
        dq = (dq * SCALE).astype(jnp.bfloat16)
        for core in range(2):
            for member in range(2):
                row = member * TILE + core * ROWS
                dqs[i, 2 * j + core, member] = dq[row : row + ROWS]

    def result_args(i, side, o):
        return (
            rs.at[i, side, o], rr.at[zh, group * PIECES + i],
            r_send.at[i, side, o], r_recv.at[zh, group * PIECES + i], owner(i, o, side),
        )

    def dq_args(i, o):
        return (
            dqs.at[i, o], dqr.at[pl.ds(group * 4 + 2 * i, 2)],
            dq_send.at[i, o], dq_recv.at[group * PIECES + i], owner(i, o, zh),
        )

    def results(i, half):
        for side in range(2):
            for o in range(4 * half, 4 * half + 4):
                at = WINDOW + (o // 2) * 256 + side * 128 + (o % 2) * ROWS
                for kind in range(2):
                    part = acc[i, kind, at : at + ROWS, :]
                    if half:
                        part = part + hr[i, kind, at - BLOCK : at - BLOCK + ROWS, :].astype(jnp.float32)
                    if kind == 0:
                        part = part * SCALE
                    rs[i, side, o, kind] = part.astype(jnp.bfloat16)
        each(4, lambda n: send(*result_args(i, zh, 4 * half + n)))

    def cross_results(i, half):
        each(4, lambda n: remote(*result_args(i, other, 4 * half + n)).start())

    def halo(i):
        return remote(
            kvx.at[i, :, pl.ds(BLOCK, WINDOW), :], kvx.at[i, :, pl.ds(0, WINDOW), :],
            halo_send.at[i], halo_recv.at[i], afters[i],
        )

    def back(i):
        return remote(hs.at[i], hr.at[i], back_send.at[i], back_recv.at[i], befores[i])

    def fetch(i):
        each(GROUPS, lambda n: arrived(kvx.at[i, :, pl.ds(0, ROWS), :], kv_recv.at[i, n]))
        each(GROUPS, lambda n: arrived(kvx.at[i, :, pl.ds(0, ROWS), :], x_recv.at[i, n]))

        @pl.when(jnp.logical_not(lasts[i]))
        def _():
            halo(i).start()

    def work(i):
        each(GROUPS, lambda n: arrived(qgx.at[pl.ds(0, 2), :, pl.ds(0, ROWS), :], qg_recv.at[i, n]))
        acc[i] = jnp.zeros(acc.shape[1:], jnp.float32)
        tile(i, 3)
        tile(i, 2)

        @pl.when(jnp.logical_not(firsts[i]))
        def _():
            arrived(kvx.at[i, :, pl.ds(0, WINDOW), :], halo_recv.at[i])

        tile(i, 1)
        tile(i, 0)
        hs[i] = acc[i, :, :WINDOW, :].astype(jnp.bfloat16)

        @pl.when(jnp.logical_not(firsts[i]))
        def _():
            back(i).start()

        results(i, 0)
        each(GROUPS, lambda n: send(*dq_args(i, n)))

    def rest(i):
        @pl.when(jnp.logical_not(lasts[i]))
        def _():
            arrived(hr.at[i], back_recv.at[i])

        results(i, 1)
        cross_results(i, 1)

    fetch(0)

    @pl.when(held)
    def _():
        each(GROUPS, early)

    work(0)

    cross_results(0, 0)
    fetch(1)
    rest(0)
    work(1)
    cross_results(1, 0)
    rest(1)

    for i in range(PIECES):
        for g in range(GROUPS):
            h = g * PIECES + i
            arrived(dqr.at[pl.ds(2 * h, 2)], dq_recv.at[h])
            for member in range(2):
                at = (2 * h + member) * HEAD
                dq_ref[:, at : at + HEAD] = dqr[2 * h + member]
            arrived(rr.at[0, h], r_recv.at[0, h])
            arrived(rr.at[1, h], r_recv.at[1, h])
            total = (rr[0, h].astype(jnp.float32) + rr[1, h].astype(jnp.float32)).astype(jnp.bfloat16)
            dk_ref[:, h * HEAD : (h + 1) * HEAD] = total[0]
            dv_ref[:, h * HEAD : (h + 1) * HEAD] = total[1]

    for i in range(PIECES):
        def finish(n):
            cross(i, n).wait_send()
            sent(*kv_args(i, n))
            sent(*qg_args(i, n))
            remote(*result_args(i, other, n)).wait_send()
            sent(*result_args(i, zh, n))
            sent(*dq_args(i, n))

        each(GROUPS, finish)

        @pl.when(jnp.logical_not(lasts[i]))
        def _():
            halo(i).wait_send()

        @pl.when(jnp.logical_not(firsts[i]))
        def _():
            back(i).wait_send()


def shards(queries, keys, values, dout, doc_starts):
    bf16, f32 = jnp.bfloat16, jnp.float32
    dma = pltpu.SemaphoreType.DMA
    return tuple(
        pl.pallas_call(
            kernel,
            out_shape=(
                jax.ShapeDtypeStruct(queries.shape, bf16),
                jax.ShapeDtypeStruct(keys.shape, bf16),
                jax.ShapeDtypeStruct(values.shape, bf16),
            ),
            in_specs=[pl.BlockSpec(memory_space=pltpu.HBM)] * 4 + [pl.BlockSpec(memory_space=pltpu.SMEM)],
            out_specs=(pl.BlockSpec(memory_space=pltpu.VMEM),) * 3,
            scratch_shapes=[
                pltpu.VMEM((ROWS, Q_HEADS * HEAD), bf16),
                pltpu.VMEM((ROWS, KV_HEADS * HEAD), bf16),
                pltpu.VMEM((ROWS, KV_HEADS * HEAD), bf16),
                pltpu.VMEM((ROWS, Q_HEADS * HEAD), bf16),
                pltpu.VMEM((KV_HEADS, 2, ROWS, HEAD), bf16),
                pltpu.VMEM((Q_HEADS, 2, ROWS, HEAD), bf16),
                pltpu.VMEM((PIECES, 2, SPAN, HEAD), bf16),
                pltpu.VMEM((4, 2, WINDOW, HEAD), bf16),
                pltpu.VMEM((PIECES, 4, 8, 2 * TILE), jnp.int32),
                pltpu.VMEM((PIECES, 2, SPAN, HEAD), f32),
                pltpu.VMEM((PIECES, 2, WINDOW, HEAD), bf16),
                pltpu.VMEM((PIECES, 2, WINDOW, HEAD), bf16),
                pltpu.VMEM((PIECES, 2, GROUPS, 2, ROWS, HEAD), bf16),
                pltpu.VMEM((PIECES, GROUPS, 2, ROWS, HEAD), bf16),
                pltpu.VMEM((2, KV_HEADS, 2, ROWS, HEAD), bf16),
                pltpu.VMEM((Q_HEADS, ROWS, HEAD), bf16),
                dma((4,)),
                dma((PIECES, GROUPS)), dma((PIECES, GROUPS)),
                dma((PIECES, GROUPS)), dma((PIECES, GROUPS)),
                dma((PIECES, GROUPS)), dma((PIECES, GROUPS)),
                dma((PIECES,)), dma((PIECES,)),
                dma((PIECES,)), dma((PIECES,)),
                dma((PIECES, 2, GROUPS)), dma((2, KV_HEADS)),
                dma((PIECES, GROUPS)), dma((KV_HEADS,)),
            ],
            compiler_params=pltpu.CompilerParams(
                collective_id=0, has_side_effects=True, vmem_limit_bytes=64 * 1024 * 1024
            ),
        )(queries, keys, values, dout, doc_starts)
    )


def solution(mesh):
    rows = P(("seq", "head"), None)
    return jax.shard_map(
        shards,
        mesh=mesh,
        in_specs=(rows, rows, rows, rows, P()),
        out_specs=(rows, rows, rows),
        check_vma=False,
    )
```

time: 168 us -> 139 us (0.83)
  the two profiles are of different devices: /device:TPU:63 before, /device:TPU:55 now
where the time goes in v2:
time: 139 us
  Pallas kernels  135 us (97%)
  local copies, waits for them, and re-layouts  3.66 us (3%)
    pallas_call x1, Pallas kernels, shards(): pl.pallas_call(kernel, out_shape=(jax.ShapeDtypeStruct(queries.shape, bf1...  135 us
    unnamed x7, local copies, waits for them, and re-layouts  3.66 us

profile of v2, /device:TPU:55, one launch (start us, length us, event | category | flops | bytes accessed | tf_op | source)
XLA Modules:
  0.0 138.9 jit_solution(15943792854713727522)
XLA Ops:
  0.6 134.6 %shard_map.76 = (bf16[64,4096]{1,0:T(8,128)(2,1)}, bf16[64,2048]{1,0:T(8,128)(2,1)}, bf16[64,2048]{1,0:T(8,128)(2,1)}) custom-call(bf16[64,4096]{1,0:T(8,128)(2,1)} %q_hbm.1, bf16[64,2048]{1,0:T(8,128)(2,1)} %k_hbm.1, bf16[64,2048]{1,0:T(8,128)(2,1)} %v_hbm.1, bf16[64,4096]{1,0:T(8,128)(2,1)} %g_hbm.1, s32[32]{0:T(128)} %doc_ref.1), custom_call_target="tpu_custom_call" | custom-call | tf_op jit(solution)/shard_map/pallas_call | solution.py:356
  135.2 0.0 copy-start.1
  135.2 1.9 %copy.11 = bf16[64,4096]{1,0:T(8,128)(2,1)} copy(bf16[64,4096]{1,0:T(8,128)(2,1)} %get-tuple-element.6) | data formatting | bytes 1048576
  137.1 0.0 copy-done.1
  137.1 0.0 copy-start
  137.1 0.7 copy.12
  137.8 0.3 copy-done
  138.2 0.7 copy.13
Async XLA Ops:
  135.2 1.9 %copy-start.1 = (bf16[64,2048]{1,0:T(8,128)(2,1)S(1)}, bf16[64,2048]{1,0:T(8,128)(2,1)}, u32[]{:S(2)}) copy-start(bf16[64,2048]{1,0:T(8,128)(2,1)} %get-tuple-element.7) | copy-start | bytes 786436
  137.1 1.0 copy-start

commit v3 on v2

--- a/solution.py
+++ b/solution.py
@@ -250,10 +250,8 @@
                     if kind == 0:
                         part = part * SCALE
                     rs[i, side, o, kind] = part.astype(jnp.bfloat16)
+        each(4, lambda n: remote(*result_args(i, other, 4 * half + n)).start())
         each(4, lambda n: send(*result_args(i, zh, 4 * half + n)))
-
-    def cross_results(i, half):
-        each(4, lambda n: remote(*result_args(i, other, 4 * half + n)).start())
 
     def halo(i):
         return remote(
@@ -299,7 +297,6 @@
             arrived(hr.at[i], back_recv.at[i])
 
         results(i, 1)
-        cross_results(i, 1)
 
     fetch(0)
 
@@ -309,11 +306,9 @@
 
     work(0)
 
-    cross_results(0, 0)
     fetch(1)
     rest(0)
     work(1)
-    cross_results(1, 0)
     rest(1)
 
     for i in range(PIECES):

time: 139 us -> 141 us (1.014)
  the two profiles are of different devices: /device:TPU:55 before, /device:TPU:63 now
where the time goes in v3:
time: 141 us
  Pallas kernels  137 us (97%)
  local copies, waits for them, and re-layouts  3.66 us (3%)
    pallas_call x1, Pallas kernels, shards(): pl.pallas_call(kernel, out_shape=(jax.ShapeDtypeStruct(queries.shape, bf1...  137 us
    unnamed x7, local copies, waits for them, and re-layouts  3.66 us

profile of v3, /device:TPU:63, one launch (start us, length us, event | category | flops | bytes accessed | tf_op | source)
XLA Modules:
  0.0 140.9 jit_solution(9361768821510439977)
XLA Ops:
  0.6 136.6 %shard_map.76 = (bf16[64,4096]{1,0:T(8,128)(2,1)}, bf16[64,2048]{1,0:T(8,128)(2,1)}, bf16[64,2048]{1,0:T(8,128)(2,1)}) custom-call(bf16[64,4096]{1,0:T(8,128)(2,1)} %q_hbm.1, bf16[64,2048]{1,0:T(8,128)(2,1)} %k_hbm.1, bf16[64,2048]{1,0:T(8,128)(2,1)} %v_hbm.1, bf16[64,4096]{1,0:T(8,128)(2,1)} %g_hbm.1, s32[32]{0:T(128)} %doc_ref.1), custom_call_target="tpu_custom_call" | custom-call | tf_op jit(solution)/shard_map/pallas_call | solution.py:351
  137.3 0.0 copy-start.1
  137.3 1.9 %copy.11 = bf16[64,4096]{1,0:T(8,128)(2,1)} copy(bf16[64,4096]{1,0:T(8,128)(2,1)} %get-tuple-element.6) | data formatting | bytes 1048576
  139.2 0.0 copy-done.1
  139.2 0.0 copy-start
  139.2 0.7 copy.12
  139.9 0.3 copy-done
  140.2 0.7 copy.13
Async XLA Ops:
  137.3 1.9 %copy-start.1 = (bf16[64,2048]{1,0:T(8,128)(2,1)S(1)}, bf16[64,2048]{1,0:T(8,128)(2,1)}, u32[]{:S(2)}) copy-start(bf16[64,2048]{1,0:T(8,128)(2,1)} %get-tuple-element.7) | copy-start | bytes 786436
  139.2 1.0 copy-start

commit v4 on v2

--- a/solution.py
+++ b/solution.py
@@ -147,9 +147,11 @@
 
     each(GROUPS, lambda n: cross(0, n).start())
 
+    each(2, early)
+
     @pl.when(jnp.logical_not(held))
     def _():
-        each(GROUPS, early)
+        each(GROUPS - 2, lambda n: early(n + 2))
 
     def kv_args(i, n):
         g = (n + group) & (GROUPS - 1)
@@ -305,7 +307,7 @@
 
     @pl.when(held)
     def _():
-        each(GROUPS, early)
+        each(GROUPS - 2, lambda n: early(n + 2))
 
     work(0)
 

time: 139 us -> 147 us (1.058)
  the two profiles are of different devices: /device:TPU:55 before, /device:TPU:49 now
where the time goes in v4:
time: 147 us
  Pallas kernels  142 us (97%)
  local copies, waits for them, and re-layouts  3.66 us (2%)
    pallas_call x1, Pallas kernels, shards(): pl.pallas_call(kernel, out_shape=(jax.ShapeDtypeStruct(queries.shape, bf1...  142 us
    unnamed x7, local copies, waits for them, and re-layouts  3.66 us

profile of v4, /device:TPU:49, one launch (start us, length us, event | category | flops | bytes accessed | tf_op | source)
XLA Modules:
  0.0 146.8 jit_solution(15930731396307924118)
XLA Ops:
  0.6 142.5 %shard_map.76 = (bf16[64,4096]{1,0:T(8,128)(2,1)}, bf16[64,2048]{1,0:T(8,128)(2,1)}, bf16[64,2048]{1,0:T(8,128)(2,1)}) custom-call(bf16[64,4096]{1,0:T(8,128)(2,1)} %q_hbm.1, bf16[64,2048]{1,0:T(8,128)(2,1)} %k_hbm.1, bf16[64,2048]{1,0:T(8,128)(2,1)} %v_hbm.1, bf16[64,4096]{1,0:T(8,128)(2,1)} %g_hbm.1, s32[32]{0:T(128)} %doc_ref.1), custom_call_target="tpu_custom_call" | custom-call | tf_op jit(solution)/shard_map/pallas_call | solution.py:358
  143.1 0.0 copy-start.1
  143.1 1.9 %copy.11 = bf16[64,4096]{1,0:T(8,128)(2,1)} copy(bf16[64,4096]{1,0:T(8,128)(2,1)} %get-tuple-element.6) | data formatting | bytes 1048576
  145.0 0.0 copy-done.1
  145.0 0.0 copy-start
  145.0 0.7 copy.12
  145.7 0.3 copy-done
  146.1 0.7 copy.13
Async XLA Ops:
  143.1 1.9 %copy-start.1 = (bf16[64,2048]{1,0:T(8,128)(2,1)S(1)}, bf16[64,2048]{1,0:T(8,128)(2,1)}, u32[]{:S(2)}) copy-start(bf16[64,2048]{1,0:T(8,128)(2,1)} %get-tuple-element.7) | copy-start | bytes 786436
  145.0 1.0 copy-start
